TPU v7x, 32 devices: a whole 2x2x4 slice. The times are simulated.
32 devices in a mesh: row: 8 (over y, x, core), col: 4 (over z).
Axes of the slice: x: 2, y: 2, z: 4, core: 2. Of those that a mesh axis runs over, the one named last changes fastest.
Arguments:
- stiffness: bfloat16 [192, 27, 128, 128], P('row'), may hold values from -1.5 to 5, as said below
- block_cols: int32 [192, 27], P('row'), may hold values from 0 to 95, as said below
- block_row_counts: int32 [8], replicated, may hold values from 1 to 24, as said below
- start_basis: float32 [512, 24576], P('col', 'row'), may hold values from -6 to 6
Outputs:
- ritz_basis: float32 [512, 24576], P('col', 'row')
- projected: float32 [512, 512], P('col')
Inputs may be any that keep to these rules, and one draw needn't show every extreme that they name: `block_cols`: on live slots the 27 entries name the global block rows coupled to that slot's block row, its own among them; dead slots hold entries of the same kind. `block_row_counts`: the counts sum to 96, and one index holds exactly 24. Over live slots the stiffness is symmetric: the blocks that couple global block rows g and h are the transposes of those that couple h and g.
All inputs are finite; a program needn't handle non-finite values.
Results may differ from a plain program's by a relative error of at most 0.013.
Values may be sent and summed in bfloat16 or wider, within the bound.
A program may use at most 128 MiB of HBM per device.

v0:
```python
import jax
import jax.numpy as jnp
from jax import lax
from jax.sharding import PartitionSpec as P

center_value = 4.0
half_width = 1.5
ridge_shift = 0.5


def transposed(left_side, right_side):
    return lax.dot_general(
        left_side,
        right_side,
        (((1,), (1,)), ((), ())),
        precision=lax.Precision.HIGHEST,
        preferred_element_type=jnp.float32,
    )


def slot_positions(columns, row_counts, slot_count):
    block_ends = jnp.cumsum(row_counts)
    block_starts = block_ends - row_counts
    owner_index = jnp.sum((block_ends[None, None, :] <= columns[:, :, None]).astype(jnp.int32), 2)
    device_ids = jnp.arange(row_counts.shape[0], dtype=jnp.int32)
    first_block = jnp.sum(
        jnp.where(
            owner_index[:, :, None] == device_ids[None, None, :], block_starts[None, None, :], 0
        ),
        2,
    )
    return owner_index * slot_count + columns - first_block


def local(stiffness, block_cols, block_row_counts, start_basis):
    slot_count = stiffness.shape[0]
    neighbours = stiffness.shape[1]
    block_size = stiffness.shape[2]
    local_modes = start_basis.shape[0]
    total_modes = local_modes * lax.axis_size("col")
    row_position = lax.axis_index("row")
    device_ids = jnp.arange(block_row_counts.shape[0], dtype=jnp.int32)
    own_count = jnp.sum(jnp.where(device_ids == row_position, block_row_counts, 0))
    live_slots = (jnp.arange(slot_count) < own_count).astype(jnp.float32)
    live_columns = jnp.repeat(live_slots, block_size)
    positions = slot_positions(block_cols, block_row_counts, slot_count).reshape(-1)
    total_dofs = (jnp.sum(block_row_counts) * block_size).astype(jnp.float32)

    def apply_stiffness(panel):
        gathered = lax.all_gather(panel, "row", axis=1, tiled=True)
        blocks = gathered.reshape(local_modes, -1, block_size)
        picked = jnp.take(blocks, positions, axis=1).reshape(
            local_modes, slot_count, neighbours, block_size
        )
        result = jnp.einsum("mpkb,pkab->mpa", picked, stiffness, preferred_element_type=jnp.float32)
        return (result * live_slots[None, :, None]).reshape(local_modes, slot_count * block_size)

    start_field = start_basis * live_columns[None, :]
    degree_one = (
        apply_stiffness(start_field.astype(jnp.bfloat16)) - center_value * start_field
    ) / half_width
    degree_two = (
        2.0
        * (apply_stiffness(degree_one.astype(jnp.bfloat16)) - center_value * degree_one)
        / half_width
        - start_field
    )
    degree_three = (
        2.0
        * (apply_stiffness(degree_two.astype(jnp.bfloat16)) - center_value * degree_two)
        / half_width
        - degree_one
    )
    filtered = lax.all_gather(degree_three, "col", axis=0, tiled=True)
    identity = jnp.eye(total_modes, dtype=jnp.float32)
    gram_matrix = (
        lax.psum(transposed(filtered, filtered), "row") / total_dofs + ridge_shift * identity
    )
    lower_factor = jnp.linalg.cholesky(gram_matrix)
    inverse = lax.linalg.triangular_solve(lower_factor, identity, left_side=True, lower=True)
    mode_start = lax.axis_index("col") * local_modes
    ritz_whole = jnp.dot(
        inverse, filtered, precision=lax.Precision.HIGHEST, preferred_element_type=jnp.float32
    )
    ritz_local = lax.dynamic_slice_in_dim(ritz_whole, mode_start, local_modes, 0)
    stiff_image = apply_stiffness(ritz_local.astype(jnp.bfloat16))
    projected = (
        lax.psum(transposed(stiff_image, ritz_whole).astype(jnp.bfloat16), "row").astype(
            jnp.float32
        )
        / total_dofs
    )
    return (ritz_local, projected)


def solution(mesh):
    in_specs = (P("row", None, None, None), P("row", None), P(), P("col", "row"))
    out_specs = (P("col", "row"), P("col", None))
    return jax.shard_map(local, mesh=mesh, in_specs=in_specs, out_specs=out_specs, check_vma=False)
```

profile of v0, /device:TPU:0, one launch (start us, length us, event | category | flops | bytes accessed | tf_op | source)
XLA Modules:
  0.0 872.0 jit_solution(9747416965826072446)
XLA Ops:
  13.8 48.0 %all-gather.6.cloned.1.call-done = bf16[128,24576]{0,1:T(8,128)(2,1)} async-done(((bf16[128,3072]{0,1:T(8,128)(2,1)}), bf16[128,24576]{0,1:T(8,128)(2,1)}) %all-gather.6.cloned.1.call-update) | async-done | bytes 6291472 | tf_op jit(solution)/shard_map/all_gather | solution.py:50
  70.4 20.8 %gather_fusion = bf16[648,128,128]{2,1,0:T(8,128)(2,1)} fusion(bf16[128,192,128]{2,0,1:T(8,128)(2,1)} %copy.26, s32[1024]{0:T(1024)S(1)} %pad_clamp_fusion), kind=kCustom, calls=%fused_computation.clone | custom fusion | bytes 42469920 | tf_op jit(solution)/shard_map/jit(_take)/gather | solution.py:52
  91.2 18.2 %broadcast_select_fusion.1 = bf16[648,128,128]{2,1,0:T(8,128)(2,1)} fusion(bf16[648,128,128]{2,1,0:T(8,128)(2,1)} %gather_fusion, pred[648]{0:T(1024)(128)(4,1)S(1)} %compare_and_fusion), kind=kLoop, calls=%fused_computation.7 | loop fusion | flops 10616832 | bytes 42467976 | tf_op jit(solution)/shard_map/jit(_take)/select_n | solution.py:52
  109.5 15.5 %bitcast_multiply_fusion.3 = f32[24,128,128]{1,2,0:T(8,128)S(1)} fusion(bf16[128,24,27,128]{3,0,2,1:T(8,128)(2,1)} %bitcast.132, bf16[24,27,128,128]{3,2,1,0:T(8,128)(2,1)} %param.6, f32[24]{0:T(128)S(1)} %compare_convert_fusion), kind=kOutput, calls=%fused_computation.21 | convolution fusion | flops 2718302208 | bytes 44040288 | tf_op jit(solution)/shard_map/mpkb,pkab->mpa/dot_general | solution.py:55
  126.6 45.4 %all-gather.8.cloned.1.call-done = bf16[128,24576]{0,1:T(8,128)(2,1)} async-done(((bf16[128,3072]{0,1:T(8,128)(2,1)}), bf16[128,24576]{0,1:T(8,128)(2,1)}) %all-gather.8.cloned.1.call-update) | async-done | bytes 6291472 | tf_op jit(solution)/shard_map/all_gather | solution.py:50
  180.6 20.8 %gather_fusion.1 = bf16[648,128,128]{2,1,0:T(8,128)(2,1)} fusion(bf16[128,192,128]{2,0,1:T(8,128)(2,1)} %copy.27, s32[1024]{0:T(1024)S(1)} %pad_clamp_fusion), kind=kCustom, calls=%fused_computation.1.clone | custom fusion | bytes 42469920 | tf_op jit(solution)/shard_map/jit(_take)/gather | solution.py:52
  201.5 18.2 %broadcast_select_fusion.2 = bf16[648,128,128]{2,1,0:T(8,128)(2,1)} fusion(bf16[648,128,128]{2,1,0:T(8,128)(2,1)} %gather_fusion.1, pred[648]{0:T(1024)(128)(4,1)S(1)} %compare_and_fusion), kind=kLoop, calls=%fused_computation.8 | loop fusion | flops 10616832 | bytes 42467976 | tf_op jit(solution)/shard_map/jit(_take)/select_n | solution.py:52
  219.7 15.4 %bitcast_multiply_fusion.2 = f32[24,128,128]{1,2,0:T(8,128)S(1)} fusion(bf16[128,24,27,128]{3,0,2,1:T(8,128)(2,1)} %bitcast.133, bf16[24,27,128,128]{3,2,1,0:T(8,128)(2,1)} %param.6, f32[24]{0:T(128)S(1)} %compare_convert_fusion), kind=kOutput, calls=%fused_computation.20 | convolution fusion | flops 2718302208 | bytes 44040288 | tf_op jit(solution)/shard_map/mpkb,pkab->mpa/dot_general | solution.py:55
  237.8 45.6 %all-gather.10.cloned.1.call-done = bf16[128,24576]{0,1:T(8,128)(2,1)} async-done(((bf16[128,3072]{0,1:T(8,128)(2,1)}), bf16[128,24576]{0,1:T(8,128)(2,1)}) %all-gather.10.cloned.1.call-update) | async-done | bytes 6291472 | tf_op jit(solution)/shard_map/all_gather | solution.py:50
  292.1 20.8 %gather_fusion.2 = bf16[648,128,128]{2,1,0:T(8,128)(2,1)} fusion(bf16[128,192,128]{2,0,1:T(8,128)(2,1)} %copy.28, s32[1024]{0:T(1024)S(1)} %pad_clamp_fusion), kind=kCustom, calls=%fused_computation.2.clone | custom fusion | bytes 42469920 | tf_op jit(solution)/shard_map/jit(_take)/gather | solution.py:52
  312.9 18.2 %broadcast_select_fusion.3 = bf16[648,128,128]{2,1,0:T(8,128)(2,1)} fusion(bf16[648,128,128]{2,1,0:T(8,128)(2,1)} %gather_fusion.2, pred[648]{0:T(1024)(128)(4,1)S(1)} %compare_and_fusion), kind=kLoop, calls=%fused_computation.9 | loop fusion | flops 10616832 | bytes 42467976 | tf_op jit(solution)/shard_map/jit(_take)/select_n | solution.py:52
  331.1 15.6 %bitcast_multiply_fusion.1 = f32[24,128,128]{1,2,0:T(8,128)S(1)} fusion(bf16[128,24,27,128]{3,0,2,1:T(8,128)(2,1)} %bitcast.134, bf16[24,27,128,128]{3,2,1,0:T(8,128)(2,1)} %param.6, f32[24]{0:T(128)S(1)} %compare_convert_fusion), kind=kOutput, calls=%fused_computation.19 | convolution fusion | flops 2718302208 | bytes 44040288 | tf_op jit(solution)/shard_map/mpkb,pkab->mpa/dot_general | solution.py:55
  349.2 115.0 %all-gather.12.cloned.1.call-done = f32[512,3072]{0,1:T(8,128)} async-done(((f32[128,3072]{0,1:T(8,128)}), f32[512,3072]{0,1:T(8,128)}) %all-gather.12.cloned.1.call-update) | async-done | bytes 6291472 | tf_op jit(solution)/shard_map/all_gather | solution.py:74
  464.1 14.8 %fusion.49 = f32[512,512]{1,0:T(8,128)} fusion(f32[512,3072]{0,1:T(8,128)} %all-gather.12.cloned.1.call-done), kind=kOutput, calls=%fused_computation.118 | convolution fusion | flops 9663676416 | bytes 7340032 | tf_op jit(solution)/shard_map/dot_general | solution.py:12
  480.4 53.6 %all-reduce.4.cloned.1.call-done = f32[512,512]{1,0:T(8,128)} async-done(((f32[512,512]{1,0:T(8,128)}), f32[512,512]{1,0:T(8,128)}) %all-reduce.4.cloned.1.call-update) | async-done | bytes 1048592 | tf_op jit(solution)/shard_map/psum | solution.py:77
  538.1 11.7 %cholesky.103 = f32[128,128]{1,0:T(8,128)S(1)} custom-call(f32[128,128]{1,0:T(8,128)S(1)} %cholesky.263), custom_call_target="Cholesky" | custom-call | tf_op jit(solution)/shard_map/jit(cholesky)/cholesky | solution.py:79
  609.2 11.9 %cholesky.253 = f32[128,128]{1,0:T(8,128)S(1)} custom-call(f32[128,128]{1,0:T(8,128)S(1)} %convolution_subtract_fusion.5), custom_call_target="Cholesky" | custom-call | tf_op jit(solution)/shard_map/jit(cholesky)/cholesky | solution.py:79
  635.3 40.1 %custom-call.33 = f32[4,128,128]{1,2,0:T(8,128)S(1)} custom-call(f32[4,128,128]{2,1,0:T(8,128)} %get-tuple-element.10), custom_call_target="InvertDiagBlocksLowerTriangular" | custom-call | tf_op jit(solution)/shard_map/triangular_solve | solution.py:80
  678.5 12.7 %fusion.4 = f32[512,3072]{1,0:T(8,128)S(1)} fusion(f32[512,3072]{0,1:T(8,128)} %all-gather.12.cloned.1.call-done, f32[128,512]{1,0:T(8,128)S(1)} %fusion.32, f32[128,512]{1,0:T(8,128)S(1)} %fusion.33, f32[128,512]{1,0:T(8,128)S(1)} %fusion.35, f32[128,512]{1,0:T(8,128)S(1)} %fusion.23), kind=kOutput, calls=%fused_computation.34 | convolution fusion | flops 9664462848 | bytes 13631488 | tf_op jit(solution)/shard_map/dot_general | solution.py:82
  695.9 44.4 %all-gather.14.cloned.1.call-done = bf16[128,24576]{1,0:T(8,128)(2,1)} async-done(((bf16[128,3072]{1,0:T(8,128)(2,1)}), bf16[128,24576]{1,0:T(8,128)(2,1)}) %all-gather.14.cloned.1.call-update) | async-done | bytes 6291472 | tf_op jit(solution)/shard_map/all_gather | solution.py:50
  747.5 20.8 %gather_fusion.3 = bf16[648,128,128]{2,1,0:T(8,128)(2,1)} fusion(bf16[128,192,128]{2,0,1:T(8,128)(2,1)} %copy_bitcast_fusion, s32[1024]{0:T(1024)S(1)} %pad_clamp_fusion), kind=kCustom, calls=%fused_computation.3.clone | custom fusion | bytes 42469920 | tf_op jit(solution)/shard_map/jit(_take)/gather | solution.py:52
  768.4 18.6 %broadcast_select_fusion = bf16[648,128,128]{2,1,0:T(8,128)(2,1)} fusion(bf16[648,128,128]{2,1,0:T(8,128)(2,1)} %gather_fusion.3, pred[648]{0:T(1024)(128)(4,1)S(1)} %compare_and_fusion), kind=kLoop, calls=%fused_computation.6 | loop fusion | flops 10616832 | bytes 42467976 | tf_op jit(solution)/shard_map/jit(_take)/select_n | solution.py:52
  787.0 15.6 %bitcast_multiply_fusion = f32[24,128,128]{1,2,0:T(8,128)S(1)} fusion(bf16[128,24,27,128]{3,0,2,1:T(8,128)(2,1)} %bitcast.131, bf16[24,27,128,128]{3,2,1,0:T(8,128)(2,1)} %param.6, f32[24]{0:T(128)S(1)} %compare_convert_fusion), kind=kOutput, calls=%fused_computation.18 | convolution fusion | flops 2718302208 | bytes 44040288 | tf_op jit(solution)/shard_map/mpkb,pkab->mpa/dot_general | solution.py:55
  810.0 53.1 %all-reduce.6.cloned.1.call-done = bf16[128,512]{1,0:T(8,128)(2,1)} async-done(((bf16[128,512]{1,0:T(8,128)(2,1)}), bf16[128,512]{1,0:T(8,128)(2,1)}) %all-reduce.6.cloned.1.call-update) | async-done | bytes 131088 | tf_op jit(solution)/shard_map/psum | solution.py:88
  (103 shorter events, 149.1 us)
Async XLA Ops:
  7.2 6.3 copy-start.4
  7.2 54.6 %all-gather.6.cloned.1.call-start = ((), (), s32[]{:S(2)}) async-start(), calls=%async_computation | async-start | bytes 7077888 | tf_op jit(solution)/shard_map/all_gather | solution.py:50
  13.4 158.6 %all-gather.8.cloned.1.call-start = ((), (), s32[]{:S(2)}) async-start(), calls=%async_computation.1 | async-start | bytes 7077888 | tf_op jit(solution)/shard_map/all_gather | solution.py:50
  126.3 157.1 %all-gather.10.cloned.1.call-start = ((), (), s32[]{:S(2)}) async-start(), calls=%async_computation.2 | async-start | bytes 7077888 | tf_op jit(solution)/shard_map/all_gather | solution.py:50
  235.1 1.1 copy-start.1
  237.7 226.4 %all-gather.12.cloned.1.call-start = ((), (), s32[]{:S(2)}) async-start(), calls=%async_computation.3 | async-start | bytes 7864320 | tf_op jit(solution)/shard_map/all_gather | solution.py:74
  331.1 15.6 %copy-start.2 = (f32[24,128,128]{1,2,0:T(8,128)S(1)}, f32[24,128,128]{1,2,0:T(8,128)}, u32[]{:S(2)}) copy-start(f32[24,128,128]{1,2,0:T(8,128)} %copy-done.1) | copy-start | bytes 4718596
  349.1 184.8 %all-reduce.4.cloned.1.call-start = ((), (), s32[]{:S(2)}) async-start(), calls=%async_computation.4 | async-start | bytes 2097152 | tf_op jit(solution)/shard_map/psum | solution.py:77
  479.0 261.3 %all-gather.14.cloned.1.call-start = ((), (), s32[]{:S(2)}) async-start(), calls=%async_computation.5 | async-start | bytes 7077888 | tf_op jit(solution)/shard_map/all_gather | solution.py:50
  537.1 1.0 copy-start.3
  691.2 2.7 copy-start
  695.6 167.5 %all-reduce.6.cloned.1.call-start = ((), (), s32[]{:S(2)}) async-start(), calls=%async_computation.6 | async-start | bytes 262144 | tf_op jit(solution)/shard_map/psum | solution.py:88
  768.3 34.2 %slice-start = ((s8[6291456]{0:T(1024)(128)(4,1)}), s8[4194304]{0:T(1024)(128)(4,1)S(1)}, s32[]{:S(2)}) async-start(s8[6291456]{0:T(1024)(128)(4,1)} %bitcast.135), calls=%async_computation.7 | async-start | bytes 8388608
  786.9 15.6 %slice-start.1 = ((s8[6291456]{0:T(1024)(128)(4,1)}), s8[2097152]{0:T(1024)(128)(4,1)S(1)}, s32[]{:S(2)}) async-start(s8[6291456]{0:T(1024)(128)(4,1)} %bitcast.135), calls=%async_computation.8 | async-start | bytes 4194304
Sparse Core Ops, SparseCore 0:
  13.5 48.2 all-gather.5
  126.4 45.5 all-gather.7
  237.9 45.5 all-gather.9
  349.2 114.8 all-gather.11
  479.1 54.7 all-reduce.3
  695.7 44.5 all-gather.13
  810.2 52.9 all-reduce.5
where the time goes:
time: 879 us; the launch traced here: 872 us
  waiting for transfers between devices  405 us (46%)
  other arithmetic  208 us (24%)
  local copies, waits for them, and re-layouts  134 us (15%)
  matrix products  106 us (12%)
  between operations  18.1 us (2%)
    all_gather x4, waiting for transfers between devices, apply_stiffness(): gathered = lax.all_gather(panel, 'row', axis=1, tiled=True)  183 us
    all_gather x1, waiting for transfers between devices, local(): filtered = lax.all_gather(degree_three, 'col', axis=0, tiled=True)  115 us
    gather x4, local copies, waits for them, and re-layouts, apply_stiffness(): jnp.take(blocks, positions, axis=1)  83.3 us
    another operation x14, other arithmetic, local(): lower_factor = jnp.linalg.cholesky(gram_matrix)  78.8 us
    select_n x5, other arithmetic, apply_stiffness(): jnp.take(blocks, positions, axis=1)  73.3 us
    dot_general x4, matrix products, apply_stiffness(): jnp.einsum('mpkb,pkab->mpa', picked, stiffness, preferred_element_type=jn...  62.1 us
    psum x1, waiting for transfers between devices, local(): lax.psum(transposed(filtered, filtered), 'row') / total_dofs  53.6 us
    psum x1, waiting for transfers between devices, local(): lax.psum(transposed(stiff_image, ritz_whole).astype(jnp.bfloat16), 'row')  53.1 us
  transfers between devices with their start and end apart: 7, of which 7 were waited for; matrix products, arithmetic and copies ran while one was open for 0% of the time, Pallas kernels for 0%

commit v1 on v0

v1 whole, which is shorter than its diff:
```python
import functools

import jax
import jax.numpy as jnp
from jax import lax
from jax.experimental import pallas as pl
from jax.experimental.pallas import tpu as pltpu
from jax.sharding import PartitionSpec as P

center_value = 4.0
half_width = 1.5
ridge_shift = 0.5

MESH = pl.DeviceIdType.MESH
HIGH = lax.Precision.HIGHEST
NT = (((1,), (1,)), ((), ()))
NN = (((1,), (0,)), ((), ()))


def gather_kernel(slots, own_ref, out_ref, send_sems, recv_sems, local_sem):
    me = lax.axis_index("row")
    half = slots // 2
    core = me % 2
    along_x = (me // 2) % 2
    along_y = me // 4
    mate = me + 1 - 2 * core
    beside = me + 2 - 4 * along_x
    above = me + 4 - 8 * along_y
    across = beside + 4 - 8 * along_y

    barrier = pltpu.get_barrier_semaphore()
    for other in (mate, beside, above):
        pl.semaphore_signal(barrier, inc=1, device_id={"row": other}, device_id_type=MESH)
    pl.semaphore_wait(barrier, 3)

    def place(device, part):
        return out_ref.at[pl.ds(device * slots + part * half, half)]

    def own(part):
        return own_ref.at[pl.ds(part * half, half)]

    def send(number, source, device, part, target):
        return pltpu.make_async_remote_copy(
            src_ref=source,
            dst_ref=place(device, part),
            send_sem=send_sems.at[number],
            recv_sem=recv_sems.at[number],
            device_id={"row": target},
            device_id_type=MESH,
        )

    copies = [
        send(0, own(0), me, 0, beside),
        send(1, own(1), me, 1, beside),
        send(2, own(0), me, 0, above),
        send(3, own(1), me, 1, above),
        send(4, place(beside, 0), beside, 0, above),
        send(5, place(above, 1), above, 1, beside),
        send(6, own(0), me, 0, mate),
        send(7, own(1), me, 1, mate),
        send(8, place(beside, 0), beside, 0, mate),
        send(9, place(beside, 1), beside, 1, mate),
        send(10, place(above, 0), above, 0, mate),
        send(11, place(above, 1), above, 1, mate),
        send(12, place(across, 0), across, 0, mate),
        send(13, place(across, 1), across, 1, mate),
    ]
    for number in (0, 3, 1, 2, 6, 7):
        copies[number].start()
    keep = pltpu.make_async_copy(own_ref, out_ref.at[pl.ds(me * slots, slots)], local_sem)
    keep.start()
    for arrived, onward in ((0, (4, 8)), (3, (5, 11)), (1, (9,)), (2, (10,)), (4, (12,)), (5, (13,))):
        copies[arrived].wait_recv()
        for number in onward:
            copies[number].start()
    for number in range(6, 14):
        copies[number].wait_recv()
    keep.wait()
    for copy in copies:
        copy.wait_send()


def gather_rows(panel):
    slots, modes, size = panel.shape
    rows = lax.axis_size("row")
    if rows != 8:
        return lax.all_gather(panel, "row", axis=0, tiled=True)
    return pl.pallas_call(
        functools.partial(gather_kernel, slots),
        out_shape=jax.ShapeDtypeStruct((rows * slots, modes, size), panel.dtype),
        in_specs=[pl.BlockSpec(memory_space=pl.ANY)],
        out_specs=pl.BlockSpec(memory_space=pl.ANY),
        scratch_shapes=[
            pltpu.SemaphoreType.DMA((14,)),
            pltpu.SemaphoreType.DMA((14,)),
            pltpu.SemaphoreType.DMA,
        ],
        compiler_params=pltpu.CompilerParams(collective_id=0, has_side_effects=True),
        name="gather_rows",
    )(panel)


def product(positions, blocks_ref, stiff_ref):
    slot = pl.program_id(0)
    neighbours = stiff_ref.shape[1]
    picked = jnp.concatenate([blocks_ref[positions[slot, k]] for k in range(neighbours)], axis=1)
    stored = jnp.concatenate([stiff_ref[0, k] for k in range(neighbours)], axis=1)
    return lax.dot_general(picked, stored, NT, preferred_element_type=jnp.float32)


def step_kernel(scale, positions, own_count, blocks_ref, stiff_ref, now_ref, before_ref, out_ref, copy_ref):
    live = pl.program_id(0) < own_count[0]

    @pl.when(live)
    def _():
        now = now_ref[0]
        result = (product(positions, blocks_ref, stiff_ref) - center_value * now) * (scale / half_width)
        if scale == 2.0:
            result = result - before_ref[0]
        out_ref[0] = result
        copy_ref[0] = result.astype(copy_ref.dtype)

    @pl.when(jnp.logical_not(live))
    def _():
        out_ref[...] = jnp.zeros_like(out_ref)
        copy_ref[...] = jnp.zeros_like(copy_ref)


def last_kernel(positions, own_count, blocks_ref, stiff_ref, now_ref, all_ref, out_ref):
    slot = pl.program_id(0)

    @pl.when(slot == 0)
    def _():
        out_ref[...] = jnp.zeros_like(out_ref)

    @pl.when(slot < own_count[0])
    def _():
        image = product(positions, blocks_ref, stiff_ref).astype(jnp.bfloat16)
        left = jnp.concatenate([now_ref[0], image], axis=0)
        whole = all_ref[...].reshape(-1, all_ref.shape[-1])
        out_ref[...] += lax.dot_general(left, whole, NT, preferred_element_type=jnp.float32)


def apply_call(kernel, positions, own_count, blocks, stiffness, extra, extra_specs, out_shape, out_specs):
    slots, neighbours, size, _ = stiffness.shape
    last = lambda slot, pos, count: (jnp.minimum(slot, count[0] - 1), 0, 0, 0)
    return pl.pallas_call(
        kernel,
        grid_spec=pltpu.PrefetchScalarGridSpec(
            num_scalar_prefetch=2,
            grid=(slots,),
            in_specs=[
                pl.BlockSpec(memory_space=pltpu.VMEM),
                pl.BlockSpec((1, neighbours, size, size), last),
                *extra_specs,
            ],
            out_specs=out_specs,
        ),
        out_shape=out_shape,
        compiler_params=pltpu.CompilerParams(vmem_limit_bytes=40 * 2**20),
    )(positions, own_count, blocks, stiffness, *extra)


def eliminate(block_ref, work_ref):
    size = block_ref.shape[0]
    rows = lax.broadcasted_iota(jnp.int32, (size, size), 0)
    columns = lax.broadcasted_iota(jnp.int32, (size, size), 1)
    work_ref[...] = (rows == columns).astype(jnp.float32)
    down = lax.broadcasted_iota(jnp.int32, (size, 1), 0)
    across = lax.broadcasted_iota(jnp.int32, (1, size), 1)

    def step(k, carry):
        pivot_row = block_ref[pl.ds(k, 1), :]
        work_row = work_ref[pl.ds(k, 1), :]
        pivot = jnp.sum(jnp.where(across == k, pivot_row, 0.0), axis=1, keepdims=True)
        root = lax.rsqrt(pivot)
        block = block_ref[...]
        column = jnp.sum(jnp.where(columns == k, block, 0.0), axis=1, keepdims=True)
        factor = jnp.where(down > k, column * (root * root), 0.0)
        block_ref[...] = block - factor * pivot_row
        work_ref[...] = jnp.where(down == k, work_ref[...] * root, work_ref[...] - factor * work_row)
        return carry

    lax.fori_loop(0, size, step, 0)


def dot(a, b, dims=NN):
    return lax.dot_general(a, b, dims, precision=HIGH, preferred_element_type=jnp.float32)


def factor_kernel(gram_ref, inverse_ref, trail, block_ref, work_ref):
    modes = gram_ref.shape[0]
    size = block_ref.shape[0]
    trail[...] = gram_ref[...]
    inverse_ref[...] = jnp.zeros_like(inverse_ref)
    for start in range(0, modes, size):
        end = start + size
        block_ref[...] = trail[start:end, start:end]
        eliminate(block_ref, work_ref)
        own = work_ref[...]
        inverse_ref[start:end, start:end] = own
        if start:
            left = dot(trail[start:end, :start], inverse_ref[:start, :start])
            inverse_ref[start:end, :start] = -dot(own, left)
        if end < modes:
            panel = dot(trail[end:, start:end], own, NT)
            trail[end:, start:end] = panel
            trail[end:, end:] = trail[end:, end:] - dot(panel, panel, NT)


def factor_inverse(gram):
    modes = gram.shape[0]
    return pl.pallas_call(
        factor_kernel,
        out_shape=jax.ShapeDtypeStruct((modes, modes), jnp.float32),
        in_specs=[pl.BlockSpec(memory_space=pltpu.VMEM)],
        out_specs=pl.BlockSpec(memory_space=pltpu.VMEM),
        scratch_shapes=[
            pltpu.VMEM((modes, modes), jnp.float32),
            pltpu.VMEM((128, 128), jnp.float32),
            pltpu.VMEM((128, 128), jnp.float32),
        ],
        compiler_params=pltpu.CompilerParams(vmem_limit_bytes=32 * 2**20),
        name="factor_inverse",
    )(gram)


def ritz_kernel(rows_ref, all_ref, out_ref):
    whole = all_ref[...].reshape(-1, all_ref.shape[-1])
    out_ref[...] = lax.dot_general(rows_ref[...], whole, NN, preferred_element_type=jnp.float32)


def local(stiffness, block_cols, block_row_counts, start_basis):
    slots, neighbours, size, _ = stiffness.shape
    modes = start_basis.shape[0]
    groups = lax.axis_size("col")
    rows = block_row_counts.shape[0]
    row_position = lax.axis_index("row")
    ids = jnp.arange(rows, dtype=jnp.int32)
    starts = jnp.sum(jnp.where(ids[None, :] < ids[:, None], block_row_counts[None, :], 0), 1)
    ends = starts + block_row_counts
    own_count = jnp.sum(jnp.where(ids == row_position, block_row_counts, 0))
    passed = (ends[None, None, :] <= block_cols[:, :, None]).astype(jnp.int32)
    owner = jnp.sum(passed, 2)
    first = jnp.sum(passed * block_row_counts[None, None, :], 2)
    positions = (owner * slots + block_cols - first).astype(jnp.int32)
    total = (jnp.sum(block_row_counts) * size).astype(jnp.float32)
    live = (jnp.arange(slots) < own_count).astype(jnp.float32)
    own_count = own_count.reshape(1)

    block = lambda: pl.BlockSpec((1, modes, size), lambda slot, pos, count: (slot, 0, 0))
    shape = (slots, modes, size)

    def advance(scale, now, now_copy, before):
        return apply_call(
            functools.partial(step_kernel, scale),
            positions,
            own_count,
            gather_rows(now_copy),
            stiffness,
            (now, before),
            [block(), block()],
            (jax.ShapeDtypeStruct(shape, jnp.float32), jax.ShapeDtypeStruct(shape, jnp.bfloat16)),
            (block(), block()),
        )

    x0 = jnp.swapaxes(start_basis.reshape(modes, slots, size), 0, 1) * live[:, None, None]
    y1, y1_copy = advance(1.0, x0, x0.astype(jnp.bfloat16), x0)
    y2, y2_copy = advance(2.0, y1, y1_copy, x0)
    y3, y3_copy = advance(2.0, y2, y2_copy, y1)

    every = lax.all_gather(y3_copy, "col", axis=0, tiled=False)
    all_modes = groups * modes
    all_block = lambda: pl.BlockSpec(
        (groups, 1, modes, size), lambda slot, *unused: (0, slot, 0, 0)
    )
    sums = apply_call(
        last_kernel,
        positions,
        own_count,
        gather_rows(y3_copy),
        stiffness,
        (y3_copy, every),
        [block(), all_block()],
        jax.ShapeDtypeStruct((2 * modes, all_modes), jnp.float32),
        pl.BlockSpec((2 * modes, all_modes), lambda slot, *unused: (0, 0)),
    )
    part = lax.psum_scatter(sums.reshape(2, rows, modes // rows, all_modes), "row", scatter_dimension=1, tiled=True)
    gram = lax.all_gather(part[0, 0], ("col", "row"), axis=0, tiled=True)
    images = lax.all_gather(part[1, 0].astype(jnp.bfloat16), ("col", "row"), axis=0, tiled=True)
    gram = gram / total + ridge_shift * jnp.eye(all_modes, dtype=jnp.float32)
    inverse = factor_inverse(gram)
    own_inverse = lax.dynamic_slice_in_dim(inverse, lax.axis_index("col") * modes, modes, 0)
    ritz = pl.pallas_call(
        ritz_kernel,
        grid=(slots,),
        in_specs=[pl.BlockSpec((modes, all_modes), lambda slot: (0, 0)), all_block()],
        out_specs=pl.BlockSpec((modes, size), lambda slot: (0, slot)),
        out_shape=jax.ShapeDtypeStruct((modes, slots * size), jnp.float32),
    )(own_inverse.astype(jnp.bfloat16), every)
    turned = dot(own_inverse, images.astype(jnp.float32))
    projected = dot(turned, inverse, NT) / total
    return (ritz, projected)


def solution(mesh):
    in_specs = (P("row", None, None, None), P("row", None), P(), P("col", "row"))
    out_specs = (P("col", "row"), P("col", None))
    return jax.shard_map(local, mesh=mesh, in_specs=in_specs, out_specs=out_specs, check_vma=False)
```

time: 879 us -> 470 us (0.53)
  waiting for transfers between devices: 405 us -> 108 us
  Pallas kernels: 0 us -> 275 us
  other arithmetic: 208 us -> 5.38 us
  local copies, waits for them, and re-layouts: 134 us -> 22.9 us
  matrix products: 106 us -> 2.26 us
  blocking collectives: 0 us -> 41.3 us
    pallas_call x0 -> x10, Pallas kernels: none -> 275 us  [the longest x4 137 us: gather_rows(): pl.pallas_call(functools.partial(gather_kernel, slots), out_shape=jax.Sha...]
    all_gather x5 -> x2, waiting for transfers between devices: 298 us -> 48.4 us  [the longest x1 36.6 us: local(): every = lax.all_gather(y3_copy, 'col', axis=0, tiled=False)]
    another operation x18 -> x0, other arithmetic: 120 us -> none  [the longest x14 78.8 us: local(): lower_factor = jnp.linalg.cholesky(gram_matrix)]
    psum x2 -> x0, waiting for transfers between devices: 107 us -> none  [the longest x1 53.6 us: local(): lax.psum(transposed(filtered, filtered), 'row') / total_dofs]
    dot_general x7 -> x2, matrix products: 97 us -> 2.26 us  [dot(): lax.dot_general(a, b, dims, precision=HIGH, preferred_element_type=jnp.fl...]
    gather x4 -> x0, local copies, waits for them, and re-layouts: 83.3 us -> none  [apply_stiffness(): jnp.take(blocks, positions, axis=1)]
    select_n x5 -> x0, other arithmetic: 73.3 us -> none  [apply_stiffness(): jnp.take(blocks, positions, axis=1)]
    unnamed x7 -> x4, waiting for transfers between devices: 0.11 us -> 59.4 us
  transfers between devices with their start and end apart: 7 -> 3, of which waited for: 7 -> 3; matrix products, arithmetic and copies ran while one was open for 0% -> 0% of each run, Pallas kernels for 0% -> 8%
where the time goes in v1:
time: 470 us; the launch traced here: 469 us
  Pallas kernels  275 us (59%)
  waiting for transfers between devices  108 us (23%)
  blocking collectives  41.3 us (9%)
  local copies, waits for them, and re-layouts  22.9 us (5%)
  between operations  14.6 us (3%)
  other arithmetic  5.38 us (1%)
    pallas_call x4, Pallas kernels, gather_rows(): pl.pallas_call(functools.partial(gather_kernel, slots), out_shape=jax.Sha...  137 us
    pallas_call x4, Pallas kernels, apply_call(): pl.pallas_call(kernel, grid_spec=pltpu.PrefetchScalarGridSpec(num_scalar_...  62.4 us
    pallas_call x1, Pallas kernels, factor_inverse(): pl.pallas_call(factor_kernel, out_shape=jax.ShapeDtypeStruct((modes, mode...  61 us
    unnamed x4, waiting for transfers between devices  59.4 us
    all_gather x1, blocking collectives, local(): lax.all_gather(part[1, 0].astype(jnp.bfloat16), ('col', 'row'), axis=0, t...  41.3 us
    all_gather x1, waiting for transfers between devices, local(): every = lax.all_gather(y3_copy, 'col', axis=0, tiled=False)  36.6 us
    unnamed x26, local copies, waits for them, and re-layouts  18.4 us
    pallas_call x1, Pallas kernels, local(): pl.pallas_call(ritz_kernel, grid=(slots,), in_specs=[pl.BlockSpec((modes,...  15 us
  transfers between devices with their start and end apart: 3, of which 3 were waited for; matrix products, arithmetic and copies ran while one was open for 0% of the time, Pallas kernels for 8%

profile of v1, /device:TPU:0, one launch (start us, length us, event | category | flops | bytes accessed | tf_op | source)
XLA Modules:
  0.0 469.3 jit_solution(979117182389080261)
XLA Ops:
  10.0 1.9 copy.10
  13.5 33.0 %gather_rows.4.blocks_ref = bf16[192,128,128]{2,1,0:T(8,128)(2,1)} custom-call(bf16[24,128,128]{2,1,0:T(8,128)(2,1)} %get-tuple-element.16.own_ref), custom_call_target="tpu_custom_call" | custom-call | tf_op jit(solution)/shard_map/gather_rows/pallas_call | solution.py:88
  46.6 2.8 copy-done
  49.4 13.1 %shard_map.59 = (f32[24,128,128]{2,1,0:T(8,128)S(1)}, bf16[24,128,128]{2,1,0:T(8,128)(2,1)S(1)}) custom-call(s32[24,27]{1,0:T(8,128)S(1)} %add_subtract_fusion.positions, s32[1]{0:T(128)} %bitcast.own_count, bf16[192,128,128]{2,1,0:T(8,128)(2,1)S(1)} %copy-done, bf16[24,27,128,128]{3,2,1,0:T(8,128)(2,1)} %stiff_ref.7, ...), custom_call_target="tpu_custom_call" | custom-call | tf_op jit(solution)/shard_map/pallas_call | solution.py:147
  63.4 32.7 %gather_rows.5.blocks_ref = bf16[192,128,128]{2,1,0:T(8,128)(2,1)} custom-call(bf16[24,128,128]{2,1,0:T(8,128)(2,1)} %copy-done.8), custom_call_target="tpu_custom_call" | custom-call | tf_op jit(solution)/shard_map/gather_rows/pallas_call | solution.py:88
  96.0 2.8 copy-done.3
  98.8 13.1 %shard_map.60 = (f32[24,128,128]{2,1,0:T(8,128)S(1)}, bf16[24,128,128]{2,1,0:T(8,128)(2,1)S(1)}) custom-call(s32[24,27]{1,0:T(8,128)S(1)} %add_subtract_fusion.positions, s32[1]{0:T(128)} %bitcast.own_count, bf16[192,128,128]{2,1,0:T(8,128)(2,1)S(1)} %copy-done.3, bf16[24,27,128,128]{3,2,1,0:T(8,128)(2,1)} %stiff_ref.7, ...), custom_call_target="tpu_custom_call" | custom-call | tf_op jit(solution)/shard_map/pallas_call | solution.py:147
  113.9 35.2 %gather_rows.6.blocks_ref = bf16[192,128,128]{2,1,0:T(8,128)(2,1)} custom-call(bf16[24,128,128]{2,1,0:T(8,128)(2,1)} %copy-done.7), custom_call_target="tpu_custom_call" | custom-call | tf_op jit(solution)/shard_map/gather_rows/pallas_call | solution.py:88
  149.2 2.8 copy-done.1
  152.0 16.9 %shard_map.61 = (f32[24,128,128]{2,1,0:T(8,128)}, bf16[24,128,128]{2,1,0:T(8,128)(2,1)}) custom-call(s32[24,27]{1,0:T(8,128)S(1)} %add_subtract_fusion.positions, s32[1]{0:T(128)} %bitcast.own_count, bf16[192,128,128]{2,1,0:T(8,128)(2,1)S(1)} %copy-done.1, bf16[24,27,128,128]{3,2,1,0:T(8,128)(2,1)} %stiff_ref.7, f32[24,128,128]{2,1,0:T(8,128)S(1)} %copy-done.6, ...), custom_call_target="tpu_custom_call" | custom-call | tf_op jit(solution)/shard_map/pallas_call | solution.py:147
  168.9 35.8 %gather_rows.7.blocks_ref = bf16[192,128,128]{2,1,0:T(8,128)(2,1)} custom-call(bf16[24,128,128]{2,1,0:T(8,128)(2,1)} %get-tuple-element.11.own_ref.now_ref), custom_call_target="tpu_custom_call" | custom-call | tf_op jit(solution)/shard_map/gather_rows/pallas_call | solution.py:88
  204.7 36.6 %all-gather.6.cloned.1.call-done = bf16[96,128,128]{2,1,0:T(8,128)(2,1)} async-done(((bf16[24,128,128]{2,1,0:T(8,128)(2,1)}), bf16[96,128,128]{2,1,0:T(8,128)(2,1)}) %all-gather.6.cloned.1.call-update) | async-done | bytes 3145744 | tf_op jit(solution)/shard_map/all_gather | solution.py:272
  241.4 2.8 copy-done.2
  244.1 1.9 copy-done.4
  246.0 19.4 %shard_map.62 = f32[256,512]{1,0:T(8,128)} custom-call(s32[24,27]{1,0:T(8,128)S(1)} %add_subtract_fusion.positions, s32[1]{0:T(128)} %bitcast.own_count, bf16[192,128,128]{2,1,0:T(8,128)(2,1)S(1)} %copy-done.2, bf16[24,27,128,128]{3,2,1,0:T(8,128)(2,1)} %stiff_ref.7, bf16[24,128,128]{2,1,0:T(8,128)(2,1)} %get-tuple-element.11.own_ref.now_ref, ...), custom_call_target="tpu_custom_call" | custom-call | tf_op jit(solution)/shard_map/pallas_call | solution.py:147
  266.1 59.4 %all-reduce.3.cloned.1.call-done = f32[2,8,16,512]{3,2,1,0:T(8,128)} async-done(((f32[2,8,16,512]{3,2,1,0:T(8,128)}), f32[2,8,16,512]{3,2,1,0:T(8,128)}) %all-reduce.3.cloned.1.call-update) | async-done | bytes 524304
  325.5 2.0 constant_dynamic-slice_fusion
  328.2 1.4 dynamic-slice_convert_fusion.1
  329.5 41.3 %all-gather.2 = bf16[1,1,512,512]{3,2,1,0:T(8,128)(2,1)S(1)} all-gather(bf16[1,1,16,512]{3,2,1,0:T(8,128)(2,1)S(1)} %dynamic-slice_convert_fusion.1), channel_id=4, replica_groups=mesh['row'=8,'col'=4] {'col','row'}, dimensions={2}, use_global_device_ids=true | all-gather | bytes 540672 | tf_op jit(solution)/shard_map/all_gather | solution.py:290
  370.8 11.8 %all-gather.8.cloned.1.call-done = f32[1,1,512,512]{3,2,1,0:T(8,128)} async-done(((f32[1,1,16,512]{3,2,1,0:T(8,128)}), f32[1,1,512,512]{3,2,1,0:T(8,128)}) %all-gather.8.cloned.1.call-update) | async-done | bytes 1048592 | tf_op jit(solution)/shard_map/all_gather | solution.py:289
  382.5 1.4 bitcast_add_fusion.gram_ref
  383.9 61.0 %factor_inverse.1 = f32[512,512]{1,0:T(8,128)S(1)} custom-call(f32[512,512]{1,0:T(8,128)S(1)} %bitcast_add_fusion.gram_ref), custom_call_target="tpu_custom_call" | custom-call | tf_op jit(solution)/shard_map/factor_inverse/pallas_call | solution.py:213
  445.9 1.9 convolution_divide_fusion
  447.8 15.0 %shard_map.63 = f32[128,3072]{1,0:T(8,128)} custom-call(bf16[128,512]{1,0:T(8,128)(2,1)} %dynamic-slice_convert_fusion.rows_ref, bf16[4,24,128,128]{3,2,1,0:T(8,128)(2,1)} %bitcast.17), custom_call_target="tpu_custom_call" | custom-call | tf_op jit(solution)/shard_map/pallas_call | solution.py:294
  (35 shorter events, 9.2 us)
Async XLA Ops:
  7.2 234.2 %all-gather.6.cloned.1.call-start = ((), (), s32[]{:S(2)}) async-start(), calls=%async_computation | async-start | bytes 3932160 | tf_op jit(solution)/shard_map/all_gather | solution.py:272
  13.5 33.0 %copy-start.9 = (s32[24,27]{1,0:T(8,128)S(1)}, s32[24,27]{1,0:T(8,128)}, u32[]{:S(2)}) copy-start(s32[24,27]{1,0:T(8,128)} %param.5) | copy-start | bytes 7780
  13.5 33.0 %copy-start.10 = (s32[8]{0:T(128)S(1)}, s32[8]{0:T(128)}, u32[]{:S(2)}) copy-start(s32[8]{0:T(128)} %param.6) | copy-start | bytes 100
  46.6 2.8 copy-start
  62.5 0.9 copy-start.8
  96.0 2.8 copy-start.3
  111.9 1.1 copy-start.5
  113.0 0.9 copy-start.7
  113.9 35.2 %copy-start.6 = (f32[24,128,128]{2,1,0:T(8,128)S(1)}, f32[24,128,128]{2,1,0:T(8,128)}, u32[]{:S(2)}) copy-start(f32[24,128,128]{2,1,0:T(8,128)} %copy-done.5) | copy-start | bytes 4718596
  149.2 2.8 copy-start.1
  168.9 156.6 %all-reduce.3.cloned.1.call-start = ((), (), s32[]{:S(2)}) async-start(), calls=%async_computation.2 | async-start | bytes 1048576
  241.4 2.8 copy-start.2
  244.1 1.9 copy-start.4
  246.0 19.5 %copy-start.11 = (u32[32]{0:T(128)S(1)}, u32[32]{0:T(128)}, u32[]{:S(2)}) copy-start(u32[32]{0:T(128)} %constant.24) | copy-start | bytes 388
  265.4 117.1 %all-gather.8.cloned.1.call-start = ((), (), s32[]{:S(2)}) async-start(), calls=%async_computation.1 | async-start | bytes 1081344 | tf_op jit(solution)/shard_map/all_gather | solution.py:289
Sparse Core Ops, SparseCore 0:
  169.0 72.2 all-gather.5
  265.6 59.8 all-reduce.2
  329.3 53.1 all-gather.7

commit v2 on v1

--- a/solution.py
+++ b/solution.py
@@ -17,7 +17,31 @@
 NN = (((1,), (0,)), ((), ()))
 
 
-def gather_kernel(slots, own_ref, out_ref, send_sems, recv_sems, local_sem):
+def line_copy(panel_ref, every_ref, sems, step, side):
+    me = lax.axis_index("col")
+    groups = every_ref.shape[0]
+    target = me + side
+    source = me - side * step
+    sends = (target >= 0) & (target < groups) & (source >= 0) & (source < groups)
+    origin = source - side
+    receives = (origin >= 0) & (origin < groups)
+    number = 2 * step + (1 if side > 0 else 0)
+    bounded = lax.rem(source + groups, groups)
+    return sends, receives, pltpu.make_async_remote_copy(
+        src_ref=panel_ref if step == 0 else every_ref.at[bounded],
+        dst_ref=every_ref.at[bounded],
+        send_sem=sems.at[0, number],
+        recv_sem=sems.at[1, number],
+        device_id={"col": lax.rem(target + groups, groups)},
+        device_id_type=MESH,
+    )
+
+
+def gather_kernel(slots, line, own_ref, out_ref, *refs):
+    if line:
+        every_ref, send_sems, recv_sems, local_sem, line_sems = refs
+    else:
+        send_sems, recv_sems, local_sem = refs
     me = lax.axis_index("row")
     half = slots // 2
     core = me % 2
@@ -31,7 +55,37 @@
     barrier = pltpu.get_barrier_semaphore()
     for other in (mate, beside, above):
         pl.semaphore_signal(barrier, inc=1, device_id={"row": other}, device_id_type=MESH)
-    pl.semaphore_wait(barrier, 3)
+    if line:
+        groups = every_ref.shape[0]
+        level = lax.axis_index("col")
+
+        @pl.when(level > 0)
+        def _():
+            pl.semaphore_signal(barrier, inc=1, device_id={"col": level - 1}, device_id_type=MESH)
+
+        @pl.when(level < groups - 1)
+        def _():
+            pl.semaphore_signal(barrier, inc=1, device_id={"col": level + 1}, device_id_type=MESH)
+
+        neighbours = (level > 0).astype(jnp.int32) + (level < groups - 1).astype(jnp.int32)
+        pl.semaphore_wait(barrier, 3 + neighbours)
+    else:
+        pl.semaphore_wait(barrier, 3)
+
+    def line_start(step):
+        for side in (-1, 1):
+            sends, _, copy = line_copy(own_ref, every_ref, line_sems, step, side)
+            pl.when(sends)(copy.start)
+
+    def line_wait(step):
+        for side in (-1, 1):
+            _, receives, copy = line_copy(own_ref, every_ref, line_sems, step, side)
+            pl.when(receives & (level - side >= 0) & (level - side < groups))(copy.wait_recv)
+
+    def line_end(step):
+        for side in (-1, 1):
+            sends, _, copy = line_copy(own_ref, every_ref, line_sems, step, side)
+            pl.when(sends)(copy.wait_send)
 
     def place(device, part):
         return out_ref.at[pl.ds(device * slots + part * half, half)]
@@ -67,37 +121,131 @@
     ]
     for number in (0, 3, 1, 2, 6, 7):
         copies[number].start()
-    keep = pltpu.make_async_copy(own_ref, out_ref.at[pl.ds(me * slots, slots)], local_sem)
-    keep.start()
-    for arrived, onward in ((0, (4, 8)), (3, (5, 11)), (1, (9,)), (2, (10,)), (4, (12,)), (5, (13,))):
+    keep = [pltpu.make_async_copy(own_ref, out_ref.at[pl.ds(me * slots, slots)], local_sem.at[0])]
+    if line:
+        line_start(0)
+        keep.append(pltpu.make_async_copy(own_ref, every_ref.at[level], local_sem.at[1]))
+    for copy in keep:
+        copy.start()
+    for arrived, onward in ((0, (4, 8)), (3, (5, 11)), (1, (9,)), (2, (10,))):
         copies[arrived].wait_recv()
         for number in onward:
             copies[number].start()
+    if line:
+        line_wait(0)
+        line_start(1)
+    for arrived, onward in ((4, 12), (5, 13)):
+        copies[arrived].wait_recv()
+        copies[onward].start()
     for number in range(6, 14):
         copies[number].wait_recv()
-    keep.wait()
+    if line:
+        for step in range(1, groups - 1):
+            line_wait(step)
+            if step < groups - 2:
+                line_start(step + 1)
+        for step in range(groups - 1):
+            line_end(step)
+    for copy in keep:
+        copy.wait()
     for copy in copies:
         copy.wait_send()
 
 
-def gather_rows(panel):
+def gather_rows(panel, number, line=False):
     slots, modes, size = panel.shape
-    rows = lax.axis_size("row")
-    if rows != 8:
-        return lax.all_gather(panel, "row", axis=0, tiled=True)
+    rows, groups = lax.axis_size("row"), lax.axis_size("col")
+    if rows != 8 or groups < 3:
+        out = lax.all_gather(panel, "row", axis=0, tiled=True)
+        return (out, lax.all_gather(panel, "col", axis=0, tiled=False)) if line else out
+    out_shape = [jax.ShapeDtypeStruct((rows * slots, modes, size), panel.dtype)]
+    scratch = [
+        pltpu.SemaphoreType.DMA((14,)),
+        pltpu.SemaphoreType.DMA((14,)),
+        pltpu.SemaphoreType.DMA((2,)),
+    ]
+    if line:
+        out_shape.append(jax.ShapeDtypeStruct((groups, slots, modes, size), panel.dtype))
+        scratch.append(pltpu.SemaphoreType.DMA((2, 2 * (groups - 1))))
+    out = pl.pallas_call(
+        functools.partial(gather_kernel, slots, line),
+        out_shape=out_shape,
+        in_specs=[pl.BlockSpec(memory_space=pl.ANY)],
+        out_specs=[pl.BlockSpec(memory_space=pl.ANY)] * len(out_shape),
+        scratch_shapes=scratch,
+        compiler_params=pltpu.CompilerParams(collective_id=number, has_side_effects=True),
+        name="gather_both" if line else "gather_rows",
+    )(panel)
+    return out if line else out[0]
+
+
+def reduce_kernel(sums_ref, out_ref, landed, total, row_sems, col_sems):
+    rows, groups = landed.shape[0], total.shape[0]
+    me, level = lax.axis_index("row"), lax.axis_index("col")
+    peers = [lax.rem(me + shift, rows) for shift in range(1, rows)]
+    levels = [lax.rem(level + shift, groups) for shift in range(1, groups)]
+    barrier = pltpu.get_barrier_semaphore()
+    for peer in peers:
+        pl.semaphore_signal(barrier, inc=1, device_id={"row": peer}, device_id_type=MESH)
+    for other in levels:
+        pl.semaphore_signal(barrier, inc=1, device_id={"col": other}, device_id_type=MESH)
+    pl.semaphore_wait(barrier, rows + groups - 2)
+    shares = []
+    for number, peer in enumerate(peers):
+        copy = pltpu.make_async_remote_copy(
+            src_ref=sums_ref.at[peer],
+            dst_ref=landed.at[number],
+            send_sem=row_sems.at[0, number],
+            recv_sem=row_sems.at[1, number],
+            device_id={"row": peer},
+            device_id_type=MESH,
+        )
+        copy.start()
+        shares.append(copy)
+    share = sums_ref[me]
+    for number, copy in enumerate(shares):
+        copy.wait_recv()
+        share = share + landed[number]
+    total[0] = share
+    out_ref[level] = share
+    exchanges = []
+    for number, other in enumerate(levels):
+        copy = pltpu.make_async_remote_copy(
+            src_ref=total.at[0],
+            dst_ref=total.at[number + 1],
+            send_sem=col_sems.at[0, number],
+            recv_sem=col_sems.at[1, number],
+            device_id={"col": other},
+            device_id_type=MESH,
+        )
+        copy.start()
+        exchanges.append(copy)
+    for number, copy in enumerate(exchanges):
+        copy.wait_recv()
+        out_ref[lax.rem(level + groups - number - 1, groups)] = total[number + 1]
+    for copy in shares + exchanges:
+        copy.wait_send()
+
+
+def reduce_sums(sums):
+    rows, groups = lax.axis_size("row"), lax.axis_size("col")
+    if rows != 8 or groups < 3:
+        share = lax.psum_scatter(sums, "row", scatter_dimension=0, tiled=False)
+        return lax.all_gather(share, "col", axis=0, tiled=False)
     return pl.pallas_call(
-        functools.partial(gather_kernel, slots),
-        out_shape=jax.ShapeDtypeStruct((rows * slots, modes, size), panel.dtype),
-        in_specs=[pl.BlockSpec(memory_space=pl.ANY)],
-        out_specs=pl.BlockSpec(memory_space=pl.ANY),
+        reduce_kernel,
+        out_shape=jax.ShapeDtypeStruct((groups, *sums.shape[1:]), sums.dtype),
+        in_specs=[pl.BlockSpec(memory_space=pltpu.VMEM)],
+        out_specs=pl.BlockSpec(memory_space=pltpu.VMEM),
         scratch_shapes=[
-            pltpu.SemaphoreType.DMA((14,)),
-            pltpu.SemaphoreType.DMA((14,)),
-            pltpu.SemaphoreType.DMA,
+            pltpu.VMEM(sums.shape, sums.dtype),
+            pltpu.VMEM((groups, *sums.shape[1:]), sums.dtype),
+            pltpu.SemaphoreType.DMA((2, rows)),
+            pltpu.SemaphoreType.DMA((2, groups)),
         ],
-        compiler_params=pltpu.CompilerParams(collective_id=0, has_side_effects=True),
-        name="gather_rows",
-    )(panel)
+        compiler_params=pltpu.CompilerParams(collective_id=3, has_side_effects=True),
+        name="reduce_sums",
+    )(sums)
 
 
 def product(positions, blocks_ref, stiff_ref):
@@ -256,7 +404,7 @@
             functools.partial(step_kernel, scale),
             positions,
             own_count,
-            gather_rows(now_copy),
+            gather_rows(now_copy, 0),
             stiffness,
             (now, before),
             [block(), block()],
@@ -269,7 +417,7 @@
     y2, y2_copy = advance(2.0, y1, y1_copy, x0)
     y3, y3_copy = advance(2.0, y2, y2_copy, y1)
 
-    every = lax.all_gather(y3_copy, "col", axis=0, tiled=False)
+    blocks, every = gather_rows(y3_copy, 1, line=True)
     all_modes = groups * modes
     all_block = lambda: pl.BlockSpec(
         (groups, 1, modes, size), lambda slot, *unused: (0, slot, 0, 0)
@@ -278,16 +426,19 @@
         last_kernel,
         positions,
         own_count,
-        gather_rows(y3_copy),
+        blocks,
         stiffness,
         (y3_copy, every),
         [block(), all_block()],
         jax.ShapeDtypeStruct((2 * modes, all_modes), jnp.float32),
         pl.BlockSpec((2 * modes, all_modes), lambda slot, *unused: (0, 0)),
     )
-    part = lax.psum_scatter(sums.reshape(2, rows, modes // rows, all_modes), "row", scatter_dimension=1, tiled=True)
-    gram = lax.all_gather(part[0, 0], ("col", "row"), axis=0, tiled=True)
-    images = lax.all_gather(part[1, 0].astype(jnp.bfloat16), ("col", "row"), axis=0, tiled=True)
+    part = modes // rows
+    shares = reduce_sums(jnp.swapaxes(sums.reshape(2, rows, part, all_modes), 0, 1))
+    shares = gather_rows(shares.reshape(groups * 2, part, all_modes), 2)
+    shares = shares.reshape(rows, groups, 2, part, all_modes)
+    gram = jnp.swapaxes(shares[:, :, 0], 0, 1).reshape(all_modes, all_modes)
+    images = jnp.swapaxes(shares[:, :, 1], 0, 1).reshape(all_modes, all_modes)
     gram = gram / total + ridge_shift * jnp.eye(all_modes, dtype=jnp.float32)
     inverse = factor_inverse(gram)
     own_inverse = lax.dynamic_slice_in_dim(inverse, lax.axis_index("col") * modes, modes, 0)
@@ -298,7 +449,7 @@
         out_specs=pl.BlockSpec((modes, size), lambda slot: (0, slot)),
         out_shape=jax.ShapeDtypeStruct((modes, slots * size), jnp.float32),
     )(own_inverse.astype(jnp.bfloat16), every)
-    turned = dot(own_inverse, images.astype(jnp.float32))
+    turned = dot(own_inverse, images)
     projected = dot(turned, inverse, NT) / total
     return (ritz, projected)
 

time: 470 us -> 376 us (0.80)
  waiting for transfers between devices: 108 us -> 0 us
  Pallas kernels: 275 us -> 339 us
  blocking collectives: 41.3 us -> 0 us
  between operations: 14.6 us -> 1.5 us
    unnamed x4 -> x0, waiting for transfers between devices: 59.4 us -> none
    all_gather x2 -> x0, waiting for transfers between devices: 48.4 us -> none  [the longest x1 36.6 us: local(): every = lax.all_gather(y3_copy, 'col', axis=0, tiled=False)]
    all_gather x1 -> x0, blocking collectives: 41.3 us -> none  [local(): lax.all_gather(part[1, 0].astype(jnp.bfloat16), ('col', 'row'), axis=0, t...]
    pallas_call x4 -> x6, Pallas kernels: 137 us -> 173 us  [the longest x5 158 us: gather_rows(): pl.pallas_call(functools.partial(gather_kernel, slots, line), out_shape=o...]
    pallas_call x4, Pallas kernels: 62.4 us -> 90.6 us  [apply_call(): pl.pallas_call(kernel, grid_spec=pltpu.PrefetchScalarGridSpec(num_scalar_...]
    unnamed x26 -> x24, local copies, waits for them, and re-layouts: 18.4 us -> 19.8 us
  transfers between devices with their start and end apart: 3 -> 0, of which waited for: 3 -> 0; matrix products, arithmetic and copies ran while one was open for 0% -> 0% of each run, Pallas kernels for 8% -> 0%
where the time goes in v2:
time: 376 us; the launch traced here: 373 us
  Pallas kernels  339 us (90%)
  local copies, waits for them, and re-layouts  23.6 us (6%)
  other arithmetic  5.61 us (1%)
    pallas_call x5, Pallas kernels, gather_rows(): pl.pallas_call(functools.partial(gather_kernel, slots, line), out_shape=o...  158 us
    pallas_call x4, Pallas kernels, apply_call(): pl.pallas_call(kernel, grid_spec=pltpu.PrefetchScalarGridSpec(num_scalar_...  90.6 us
    pallas_call x1, Pallas kernels, factor_inverse(): pl.pallas_call(factor_kernel, out_shape=jax.ShapeDtypeStruct((modes, mode...  61 us
    unnamed x24, local copies, waits for them, and re-layouts  19.8 us
    pallas_call x1, Pallas kernels, reduce_sums(): pl.pallas_call(reduce_kernel, out_shape=jax.ShapeDtypeStruct((groups, *su...  15 us
    pallas_call x1, Pallas kernels, local(): pl.pallas_call(ritz_kernel, grid=(slots,), in_specs=[pl.BlockSpec((modes,...  15 us

profile of v2, /device:TPU:0, one launch (start us, length us, event | category | flops | bytes accessed | tf_op | source)
XLA Modules:
  0.0 372.5 jit_solution(10369746485548191720)
XLA Ops:
  1.4 1.3 fusion.6
  5.6 1.9 copy.12
  7.9 1.2 fusion.7
  9.1 33.0 %gather_rows.4.blocks_ref = bf16[192,128,128]{2,1,0:T(8,128)(2,1)} custom-call(bf16[24,128,128]{2,1,0:T(8,128)(2,1)} %get-tuple-element.20.own_ref), custom_call_target="tpu_custom_call" | custom-call | tf_op jit(solution)/shard_map/gather_rows/pallas_call | solution.py:170
  42.1 2.8 copy-done.2
  44.8 21.5 %shard_map.59 = (f32[24,128,128]{2,1,0:T(8,128)S(1)}, bf16[24,128,128]{2,1,0:T(8,128)(2,1)S(1)}) custom-call(s32[24,27]{1,0:T(8,128)S(1)} %add_subtract_fusion.positions, s32[1]{0:T(128)} %bitcast.own_count, bf16[192,128,128]{2,1,0:T(8,128)(2,1)S(1)} %copy-done.2, bf16[24,27,128,128]{3,2,1,0:T(8,128)(2,1)} %stiff_ref.7, ...), custom_call_target="tpu_custom_call" | custom-call | tf_op jit(solution)/shard_map/pallas_call | solution.py:295
  67.3 26.8 %gather_rows.5.blocks_ref = bf16[192,128,128]{2,1,0:T(8,128)(2,1)} custom-call(bf16[24,128,128]{2,1,0:T(8,128)(2,1)} %copy-done.10), custom_call_target="tpu_custom_call" | custom-call | tf_op jit(solution)/shard_map/gather_rows/pallas_call | solution.py:170
  94.1 2.8 copy-done.1
  96.8 21.5 %shard_map.60 = (f32[24,128,128]{2,1,0:T(8,128)S(1)}, bf16[24,128,128]{2,1,0:T(8,128)(2,1)S(1)}) custom-call(s32[24,27]{1,0:T(8,128)S(1)} %add_subtract_fusion.positions, s32[1]{0:T(128)} %bitcast.own_count, bf16[192,128,128]{2,1,0:T(8,128)(2,1)S(1)} %copy-done.1, bf16[24,27,128,128]{3,2,1,0:T(8,128)(2,1)} %stiff_ref.7, ...), custom_call_target="tpu_custom_call" | custom-call | tf_op jit(solution)/shard_map/pallas_call | solution.py:295
  118.4 1.1 copy-done.7
  120.4 26.8 %gather_rows.6.blocks_ref = bf16[192,128,128]{2,1,0:T(8,128)(2,1)} custom-call(bf16[24,128,128]{2,1,0:T(8,128)(2,1)} %copy-done.9), custom_call_target="tpu_custom_call" | custom-call | tf_op jit(solution)/shard_map/gather_rows/pallas_call | solution.py:170
  147.2 2.8 copy-done
  150.0 22.6 %shard_map.61 = (f32[24,128,128]{2,1,0:T(8,128)}, bf16[24,128,128]{2,1,0:T(8,128)(2,1)S(1)}) custom-call(s32[24,27]{1,0:T(8,128)S(1)} %add_subtract_fusion.positions, s32[1]{0:T(128)} %bitcast.own_count, bf16[192,128,128]{2,1,0:T(8,128)(2,1)S(1)} %copy-done, bf16[24,27,128,128]{3,2,1,0:T(8,128)(2,1)} %stiff_ref.7, f32[24,128,128]{2,1,0:T(8,128)S(1)} %copy-done.8, ...), custom_call_target="tpu_custom_call" | custom-call | tf_op jit(solution)/shard_map/pallas_call | solution.py:295
  173.5 57.7 %gather_both.1 = (bf16[192,128,128]{2,1,0:T(8,128)(2,1)}, bf16[4,24,128,128]{3,2,1,0:T(8,128)(2,1)}) custom-call(bf16[24,128,128]{2,1,0:T(8,128)(2,1)} %copy-done.5), custom_call_target="tpu_custom_call" | custom-call | tf_op jit(solution)/shard_map/gather_both/pallas_call | solution.py:170
  231.2 1.9 copy-done.3
  233.1 2.8 copy-done.4
  235.9 1.1 copy-done.6
  237.0 24.9 %shard_map.62 = f32[256,512]{1,0:T(8,128)S(1)} custom-call(s32[24,27]{1,0:T(8,128)S(1)} %add_subtract_fusion.positions, s32[1]{0:T(128)} %bitcast.own_count, bf16[192,128,128]{2,1,0:T(8,128)(2,1)S(1)} %copy-done.4, bf16[24,27,128,128]{3,2,1,0:T(8,128)(2,1)} %stiff_ref.7, bf16[24,128,128]{2,1,0:T(8,128)(2,1)S(1)} %copy-done.6, ...), custom_call_target="tpu_custom_call" | custom-call | tf_op jit(solution)/shard_map/pallas_call | solution.py:295
  262.8 15.0 %reduce_sums.1 = f32[4,2,16,512]{3,2,1,0:T(8,128)} custom-call(f32[8,2,16,512]{3,2,1,0:T(8,128)} %bitcast.29), custom_call_target="tpu_custom_call" | custom-call | tf_op jit(solution)/shard_map/reduce_sums/pallas_call | solution.py:235
  277.8 13.4 %gather_rows.7 = f32[64,16,512]{2,1,0:T(8,128)} custom-call(f32[8,16,512]{2,1,0:T(8,128)} %bitcast.30), custom_call_target="tpu_custom_call" | custom-call | tf_op jit(solution)/shard_map/gather_rows/pallas_call | solution.py:170
  291.2 1.8 fusion.8
  293.3 61.0 %factor_inverse.1 = f32[512,512]{1,0:T(8,128)S(1)} custom-call(f32[512,512]{1,0:T(8,128)S(1)} %bitcast_add_fusion.gram_ref), custom_call_target="tpu_custom_call" | custom-call | tf_op jit(solution)/shard_map/factor_inverse/pallas_call | solution.py:361
  355.0 1.9 convolution_divide_fusion
  357.6 15.0 %shard_map.63 = f32[128,3072]{1,0:T(8,128)} custom-call(bf16[128,512]{1,0:T(8,128)(2,1)} %dynamic-slice_convert_fusion.rows_ref, bf16[4,24,128,128]{3,2,1,0:T(8,128)(2,1)} %get-tuple-element.15.all_ref), custom_call_target="tpu_custom_call" | custom-call | tf_op jit(solution)/shard_map/pallas_call | solution.py:445
  (26 shorter events, 8.6 us)
Async XLA Ops:
  42.1 2.8 copy-start.2
  66.4 0.9 copy-start.10
  94.1 2.8 copy-start.1
  118.4 1.1 copy-start.7
  119.5 0.9 copy-start.9
  120.4 26.8 %copy-start.8 = (f32[24,128,128]{2,1,0:T(8,128)S(1)}, f32[24,128,128]{2,1,0:T(8,128)}, u32[]{:S(2)}) copy-start(f32[24,128,128]{2,1,0:T(8,128)} %copy-done.7) | copy-start | bytes 4718596
  147.2 2.8 copy-start
  172.6 0.9 copy-start.5
  231.2 1.9 copy-start.3
  233.1 2.8 copy-start.4
  235.9 1.1 copy-start.6

commit v3 on v2

--- a/solution.py
+++ b/solution.py
@@ -336,7 +336,7 @@
     return lax.dot_general(a, b, dims, precision=HIGH, preferred_element_type=jnp.float32)
 
 
-def factor_kernel(gram_ref, inverse_ref, trail, block_ref, work_ref):
+def exact_factor(gram_ref, inverse_ref, trail, block_ref, work_ref):
     modes = gram_ref.shape[0]
     size = block_ref.shape[0]
     trail[...] = gram_ref[...]
@@ -356,6 +356,55 @@
             trail[end:, end:] = trail[end:, end:] - dot(panel, panel, NT)
 
 
+def split(a):
+    high = a.astype(jnp.bfloat16)
+    return high, (a - high.astype(jnp.float32)).astype(jnp.bfloat16)
+
+
+def one_pass(a, b, dims=NN):
+    return lax.dot_general(
+        a.astype(jnp.bfloat16), b.astype(jnp.bfloat16), dims, preferred_element_type=jnp.float32
+    )
+
+
+def three_pass(a, b, dims=NN):
+    (a_high, a_low), (b_high, b_low) = split(a), split(b)
+    go = lambda x, y: lax.dot_general(x, y, dims, preferred_element_type=jnp.float32)
+    return go(a_high, b_high) + (go(a_high, b_low) + go(a_low, b_high))
+
+
+def factor_kernel(gram_ref, inverse_ref, trail, block_ref, work_ref):
+    modes = gram_ref.shape[0]
+    down = lax.broadcasted_iota(jnp.int32, (modes, modes), 0)
+    across = lax.broadcasted_iota(jnp.int32, (modes, modes), 1)
+    diagonal = jnp.where(down == across, 1.0, 0.0)
+    weight = jnp.where(down > across, 1.0, 0.5 * diagonal)
+    trail[...] = gram_ref[...]
+    variance = jnp.sum(trail[...] * diagonal, axis=1, keepdims=True)
+    inverse_ref[...] = diagonal * lax.rsqrt(variance)
+
+    def refine(multiply, limit, most):
+        def going(state):
+            return (state[0] < most) & (state[1] > limit)
+
+        def step(state):
+            now = inverse_ref[...]
+            error = multiply(multiply(now, trail[...]), now, NT) - diagonal
+            inverse_ref[...] = now - multiply(error * weight, now)
+            return state[0] + 1, jnp.max(jnp.abs(error))
+
+        return lax.while_loop(going, step, (jnp.int32(0), jnp.float32(1e30)))[1]
+
+    refine(one_pass, 0.06, 12)
+    error = refine(three_pass, 5e-4, 6)
+    least = jnp.min(jnp.where(down == across, inverse_ref[...], 1.0))
+    good = (error <= 5e-4) & (least > 0.0)
+
+    @pl.when(jnp.logical_not(good))
+    def _():
+        exact_factor(gram_ref, inverse_ref, trail, block_ref, work_ref)
+
+
 def factor_inverse(gram):
     modes = gram.shape[0]
     return pl.pallas_call(
@@ -374,8 +423,13 @@
 
 
 def ritz_kernel(rows_ref, all_ref, out_ref):
-    whole = all_ref[...].reshape(-1, all_ref.shape[-1])
-    out_ref[...] = lax.dot_general(rows_ref[...], whole, NN, preferred_element_type=jnp.float32)
+    groups, slots, modes, size = all_ref.shape
+    rows = rows_ref[...]
+    for slot in range(slots):
+        whole = all_ref[:, slot].reshape(groups * modes, size)
+        out_ref[:, slot * size : (slot + 1) * size] = lax.dot_general(
+            rows, whole, NN, preferred_element_type=jnp.float32
+        )
 
 
 def local(stiffness, block_cols, block_row_counts, start_basis):
@@ -442,11 +496,15 @@
     gram = gram / total + ridge_shift * jnp.eye(all_modes, dtype=jnp.float32)
     inverse = factor_inverse(gram)
     own_inverse = lax.dynamic_slice_in_dim(inverse, lax.axis_index("col") * modes, modes, 0)
+    width = 4 if slots % 4 == 0 else 1
     ritz = pl.pallas_call(
         ritz_kernel,
-        grid=(slots,),
-        in_specs=[pl.BlockSpec((modes, all_modes), lambda slot: (0, 0)), all_block()],
-        out_specs=pl.BlockSpec((modes, size), lambda slot: (0, slot)),
+        grid=(slots // width,),
+        in_specs=[
+            pl.BlockSpec((modes, all_modes), lambda step: (0, 0)),
+            pl.BlockSpec((groups, width, modes, size), lambda step: (0, step, 0, 0)),
+        ],
+        out_specs=pl.BlockSpec((modes, width * size), lambda step: (0, step)),
         out_shape=jax.ShapeDtypeStruct((modes, slots * size), jnp.float32),
     )(own_inverse.astype(jnp.bfloat16), every)
     turned = dot(own_inverse, images)

time: 376 us -> 374 us (level)
    pallas_call x4, Pallas kernels: 90.6 us -> 60.6 us  [apply_call(): pl.pallas_call(kernel, grid_spec=pltpu.PrefetchScalarGridSpec(num_scalar_...]
    pallas_call x5, Pallas kernels: 158 us -> 180 us  [gather_rows(): pl.pallas_call(functools.partial(gather_kernel, slots, line), out_shape=o...]
    pallas_call x1, Pallas kernels: 15 us -> 5.6 us  [local(): pl.pallas_call(ritz_kernel, grid=(slots // width,), in_specs=[pl.BlockSpe...]
    pallas_call x1, Pallas kernels: 61 us -> 69.1 us  [factor_inverse(): pl.pallas_call(factor_kernel, out_shape=jax.ShapeDtypeStruct((modes, mode...]
    pallas_call x1, Pallas kernels: 15 us -> 22.5 us  [reduce_sums(): pl.pallas_call(reduce_kernel, out_shape=jax.ShapeDtypeStruct((groups, *su...]
where the time goes in v3:
time: 374 us; the launch traced here: 371 us
  Pallas kernels  337 us (90%)
  local copies, waits for them, and re-layouts  23.6 us (6%)
  other arithmetic  5.61 us (2%)
    pallas_call x5, Pallas kernels, gather_rows(): pl.pallas_call(functools.partial(gather_kernel, slots, line), out_shape=o...  180 us
    pallas_call x1, Pallas kernels, factor_inverse(): pl.pallas_call(factor_kernel, out_shape=jax.ShapeDtypeStruct((modes, mode...  69.1 us
    pallas_call x4, Pallas kernels, apply_call(): pl.pallas_call(kernel, grid_spec=pltpu.PrefetchScalarGridSpec(num_scalar_...  60.6 us
    pallas_call x1, Pallas kernels, reduce_sums(): pl.pallas_call(reduce_kernel, out_shape=jax.ShapeDtypeStruct((groups, *su...  22.5 us
    unnamed x24, local copies, waits for them, and re-layouts  19.8 us

profile of v3, /device:TPU:0, one launch (start us, length us, event | category | flops | bytes accessed | tf_op | source)
XLA Modules:
  0.0 370.8 jit_solution(15827078606007210538)
XLA Ops:
  1.4 1.3 fusion.6
  5.6 1.9 copy.12
  7.9 1.2 fusion.7
  9.1 33.0 %gather_rows.4.blocks_ref = bf16[192,128,128]{2,1,0:T(8,128)(2,1)} custom-call(bf16[24,128,128]{2,1,0:T(8,128)(2,1)} %get-tuple-element.20.own_ref), custom_call_target="tpu_custom_call" | custom-call | tf_op jit(solution)/shard_map/gather_rows/pallas_call | solution.py:170
  42.1 2.8 copy-done.2
  44.8 13.7 %shard_map.59 = (f32[24,128,128]{2,1,0:T(8,128)S(1)}, bf16[24,128,128]{2,1,0:T(8,128)(2,1)S(1)}) custom-call(s32[24,27]{1,0:T(8,128)S(1)} %add_subtract_fusion.positions, s32[1]{0:T(128)} %bitcast.own_count, bf16[192,128,128]{2,1,0:T(8,128)(2,1)S(1)} %copy-done.2, bf16[24,27,128,128]{3,2,1,0:T(8,128)(2,1)} %stiff_ref.7, ...), custom_call_target="tpu_custom_call" | custom-call | tf_op jit(solution)/shard_map/pallas_call | solution.py:295
  59.4 37.6 %gather_rows.5.blocks_ref = bf16[192,128,128]{2,1,0:T(8,128)(2,1)} custom-call(bf16[24,128,128]{2,1,0:T(8,128)(2,1)} %copy-done.10), custom_call_target="tpu_custom_call" | custom-call | tf_op jit(solution)/shard_map/gather_rows/pallas_call | solution.py:170
  97.0 2.8 copy-done.1
  99.8 13.6 %shard_map.60 = (f32[24,128,128]{2,1,0:T(8,128)S(1)}, bf16[24,128,128]{2,1,0:T(8,128)(2,1)S(1)}) custom-call(s32[24,27]{1,0:T(8,128)S(1)} %add_subtract_fusion.positions, s32[1]{0:T(128)} %bitcast.own_count, bf16[192,128,128]{2,1,0:T(8,128)(2,1)S(1)} %copy-done.1, bf16[24,27,128,128]{3,2,1,0:T(8,128)(2,1)} %stiff_ref.7, ...), custom_call_target="tpu_custom_call" | custom-call | tf_op jit(solution)/shard_map/pallas_call | solution.py:295
  113.5 1.1 copy-done.7
  115.5 33.6 %gather_rows.6.blocks_ref = bf16[192,128,128]{2,1,0:T(8,128)(2,1)} custom-call(bf16[24,128,128]{2,1,0:T(8,128)(2,1)} %copy-done.9), custom_call_target="tpu_custom_call" | custom-call | tf_op jit(solution)/shard_map/gather_rows/pallas_call | solution.py:170
  149.1 2.8 copy-done
  151.9 17.5 %shard_map.61 = (f32[24,128,128]{2,1,0:T(8,128)}, bf16[24,128,128]{2,1,0:T(8,128)(2,1)S(1)}) custom-call(s32[24,27]{1,0:T(8,128)S(1)} %add_subtract_fusion.positions, s32[1]{0:T(128)} %bitcast.own_count, bf16[192,128,128]{2,1,0:T(8,128)(2,1)S(1)} %copy-done, bf16[24,27,128,128]{3,2,1,0:T(8,128)(2,1)} %stiff_ref.7, f32[24,128,128]{2,1,0:T(8,128)S(1)} %copy-done.8, ...), custom_call_target="tpu_custom_call" | custom-call | tf_op jit(solution)/shard_map/pallas_call | solution.py:295
  170.2 60.9 %gather_both.1 = (bf16[192,128,128]{2,1,0:T(8,128)(2,1)}, bf16[4,24,128,128]{3,2,1,0:T(8,128)(2,1)}) custom-call(bf16[24,128,128]{2,1,0:T(8,128)(2,1)} %copy-done.5), custom_call_target="tpu_custom_call" | custom-call | tf_op jit(solution)/shard_map/gather_both/pallas_call | solution.py:170
  231.1 1.9 copy-done.3
  233.0 2.8 copy-done.4
  235.8 1.1 copy-done.6
  236.9 15.9 %shard_map.62 = f32[256,512]{1,0:T(8,128)S(1)} custom-call(s32[24,27]{1,0:T(8,128)S(1)} %add_subtract_fusion.positions, s32[1]{0:T(128)} %bitcast.own_count, bf16[192,128,128]{2,1,0:T(8,128)(2,1)S(1)} %copy-done.4, bf16[24,27,128,128]{3,2,1,0:T(8,128)(2,1)} %stiff_ref.7, bf16[24,128,128]{2,1,0:T(8,128)(2,1)S(1)} %copy-done.6, ...), custom_call_target="tpu_custom_call" | custom-call | tf_op jit(solution)/shard_map/pallas_call | solution.py:295
  253.6 22.5 %reduce_sums.1 = f32[4,2,16,512]{3,2,1,0:T(8,128)} custom-call(f32[8,2,16,512]{3,2,1,0:T(8,128)} %bitcast.29), custom_call_target="tpu_custom_call" | custom-call | tf_op jit(solution)/shard_map/reduce_sums/pallas_call | solution.py:235
  276.2 14.5 %gather_rows.7 = f32[64,16,512]{2,1,0:T(8,128)} custom-call(f32[8,16,512]{2,1,0:T(8,128)} %bitcast.30), custom_call_target="tpu_custom_call" | custom-call | tf_op jit(solution)/shard_map/gather_rows/pallas_call | solution.py:170
  290.7 1.8 fusion.8
  292.8 69.1 %factor_inverse.1 = f32[512,512]{1,0:T(8,128)S(1)} custom-call(f32[512,512]{1,0:T(8,128)S(1)} %bitcast_add_fusion.gram_ref), custom_call_target="tpu_custom_call" | custom-call | tf_op jit(solution)/shard_map/factor_inverse/pallas_call | solution.py:410
  362.6 1.9 convolution_divide_fusion
  365.2 5.6 %shard_map.63 = f32[128,3072]{1,0:T(8,128)} custom-call(bf16[128,512]{1,0:T(8,128)(2,1)} %dynamic-slice_convert_fusion.rows_ref, bf16[4,24,128,128]{3,2,1,0:T(8,128)(2,1)} %get-tuple-element.15.all_ref), custom_call_target="tpu_custom_call" | custom-call | tf_op jit(solution)/shard_map/pallas_call | solution.py:500
  (26 shorter events, 8.6 us)
Async XLA Ops:
  42.1 2.8 copy-start.2
  58.5 0.9 copy-start.10
  97.0 2.8 copy-start.1
  113.5 1.1 copy-start.7
  114.6 0.9 copy-start.9
  115.5 33.6 %copy-start.8 = (f32[24,128,128]{2,1,0:T(8,128)S(1)}, f32[24,128,128]{2,1,0:T(8,128)}, u32[]{:S(2)}) copy-start(f32[24,128,128]{2,1,0:T(8,128)} %copy-done.7) | copy-start | bytes 4718596
  149.1 2.8 copy-start
  169.4 0.9 copy-start.5
  231.1 1.9 copy-start.3
  233.0 2.8 copy-start.4
  235.8 1.1 copy-start.6

commit v4 on v3

--- a/solution.py
+++ b/solution.py
@@ -248,61 +248,83 @@
     )(sums)
 
 
-def product(positions, blocks_ref, stiff_ref):
-    slot = pl.program_id(0)
-    neighbours = stiff_ref.shape[1]
+def product(positions, slot, blocks_ref, stored_ref):
+    neighbours = stored_ref.shape[0]
     picked = jnp.concatenate([blocks_ref[positions[slot, k]] for k in range(neighbours)], axis=1)
-    stored = jnp.concatenate([stiff_ref[0, k] for k in range(neighbours)], axis=1)
+    stored = jnp.concatenate([stored_ref[k] for k in range(neighbours)], axis=1)
     return lax.dot_general(picked, stored, NT, preferred_element_type=jnp.float32)
 
 
 def step_kernel(scale, positions, own_count, blocks_ref, stiff_ref, now_ref, before_ref, out_ref, copy_ref):
-    live = pl.program_id(0) < own_count[0]
-
-    @pl.when(live)
-    def _():
-        now = now_ref[0]
-        result = (product(positions, blocks_ref, stiff_ref) - center_value * now) * (scale / half_width)
-        if scale == 2.0:
-            result = result - before_ref[0]
-        out_ref[0] = result
-        copy_ref[0] = result.astype(copy_ref.dtype)
-
-    @pl.when(jnp.logical_not(live))
+    width = stiff_ref.shape[0]
+
+    def one(i, slot):
+        @pl.when(slot < own_count[0])
+        def _():
+            now = now_ref[i]
+            result = product(positions, slot, blocks_ref, stiff_ref.at[i]) - center_value * now
+            result = result * (scale / half_width)
+            if scale == 2.0:
+                result = result - before_ref[i]
+            out_ref[i] = result
+            copy_ref[i] = result.astype(copy_ref.dtype)
+
+        @pl.when(slot >= own_count[0])
+        def _():
+            out_ref[i] = jnp.zeros(out_ref.shape[1:], out_ref.dtype)
+            copy_ref[i] = jnp.zeros(copy_ref.shape[1:], copy_ref.dtype)
+
+    for i in range(width):
+        one(i, pl.program_id(0) * width + i)
+
+
+def last_kernel(positions, own_count, blocks_ref, stiff_ref, now_ref, all_ref, out_ref, left_ref):
+    groups, width, modes, size = all_ref.shape
+    first = pl.program_id(0) * width
+
+    @pl.when(first == 0)
     def _():
         out_ref[...] = jnp.zeros_like(out_ref)
-        copy_ref[...] = jnp.zeros_like(copy_ref)
-
-
-def last_kernel(positions, own_count, blocks_ref, stiff_ref, now_ref, all_ref, out_ref):
-    slot = pl.program_id(0)
-
-    @pl.when(slot == 0)
+
+    def one(i, slot):
+        left_ref[:modes, i * size : (i + 1) * size] = now_ref[i]
+
+        @pl.when(slot < own_count[0])
+        def _():
+            image = product(positions, slot, blocks_ref, stiff_ref.at[i])
+            left_ref[modes:, i * size : (i + 1) * size] = image.astype(left_ref.dtype)
+
+        @pl.when(slot >= own_count[0])
+        def _():
+            left_ref[modes:, i * size : (i + 1) * size] = jnp.zeros((modes, size), left_ref.dtype)
+
+    @pl.when(first < own_count[0])
     def _():
-        out_ref[...] = jnp.zeros_like(out_ref)
-
-    @pl.when(slot < own_count[0])
-    def _():
-        image = product(positions, blocks_ref, stiff_ref).astype(jnp.bfloat16)
-        left = jnp.concatenate([now_ref[0], image], axis=0)
-        whole = all_ref[...].reshape(-1, all_ref.shape[-1])
-        out_ref[...] += lax.dot_general(left, whole, NT, preferred_element_type=jnp.float32)
-
-
-def apply_call(kernel, positions, own_count, blocks, stiffness, extra, extra_specs, out_shape, out_specs):
+        for i in range(width):
+            one(i, first + i)
+        whole = jnp.concatenate(
+            [all_ref[:, i].reshape(groups * modes, size) for i in range(width)], axis=1
+        )
+        out_ref[...] += lax.dot_general(left_ref[...], whole, NT, preferred_element_type=jnp.float32)
+
+
+def apply_call(
+    kernel, width, positions, own_count, blocks, stiffness, extra, extra_specs, out_shape, out_specs, scratch=()
+):
     slots, neighbours, size, _ = stiffness.shape
-    last = lambda slot, pos, count: (jnp.minimum(slot, count[0] - 1), 0, 0, 0)
+    last = lambda step, pos, count: (jnp.minimum(step, lax.div(count[0] - 1, width)), 0, 0, 0)
     return pl.pallas_call(
         kernel,
         grid_spec=pltpu.PrefetchScalarGridSpec(
             num_scalar_prefetch=2,
-            grid=(slots,),
+            grid=(slots // width,),
             in_specs=[
                 pl.BlockSpec(memory_space=pltpu.VMEM),
-                pl.BlockSpec((1, neighbours, size, size), last),
+                pl.BlockSpec((width, neighbours, size, size), last),
                 *extra_specs,
             ],
             out_specs=out_specs,
+            scratch_shapes=list(scratch),
         ),
         out_shape=out_shape,
         compiler_params=pltpu.CompilerParams(vmem_limit_bytes=40 * 2**20),
@@ -450,12 +472,14 @@
     live = (jnp.arange(slots) < own_count).astype(jnp.float32)
     own_count = own_count.reshape(1)
 
-    block = lambda: pl.BlockSpec((1, modes, size), lambda slot, pos, count: (slot, 0, 0))
+    width = 4 if slots % 4 == 0 else 1
+    block = lambda: pl.BlockSpec((width, modes, size), lambda slot, pos, count: (slot, 0, 0))
     shape = (slots, modes, size)
 
     def advance(scale, now, now_copy, before):
         return apply_call(
             functools.partial(step_kernel, scale),
+            width,
             positions,
             own_count,
             gather_rows(now_copy, 0),
@@ -474,10 +498,11 @@
     blocks, every = gather_rows(y3_copy, 1, line=True)
     all_modes = groups * modes
     all_block = lambda: pl.BlockSpec(
-        (groups, 1, modes, size), lambda slot, *unused: (0, slot, 0, 0)
+        (groups, width, modes, size), lambda slot, *unused: (0, slot, 0, 0)
     )
     sums = apply_call(
         last_kernel,
+        width,
         positions,
         own_count,
         blocks,
@@ -486,6 +511,7 @@
         [block(), all_block()],
         jax.ShapeDtypeStruct((2 * modes, all_modes), jnp.float32),
         pl.BlockSpec((2 * modes, all_modes), lambda slot, *unused: (0, 0)),
+        (pltpu.VMEM((2 * modes, width * size), jnp.bfloat16),),
     )
     part = modes // rows
     shares = reduce_sums(jnp.swapaxes(sums.reshape(2, rows, part, all_modes), 0, 1))
@@ -496,7 +522,6 @@
     gram = gram / total + ridge_shift * jnp.eye(all_modes, dtype=jnp.float32)
     inverse = factor_inverse(gram)
     own_inverse = lax.dynamic_slice_in_dim(inverse, lax.axis_index("col") * modes, modes, 0)
-    width = 4 if slots % 4 == 0 else 1
     ritz = pl.pallas_call(
         ritz_kernel,
         grid=(slots // width,),

time: 374 us -> 343 us (0.917)
  Pallas kernels: 337 us -> 308 us
    pallas_call x4, Pallas kernels: 60.6 us -> 34.9 us  [apply_call(): pl.pallas_call(kernel, grid_spec=pltpu.PrefetchScalarGridSpec(num_scalar_...]
    pallas_call x5, Pallas kernels: 180 us -> 174 us  [gather_rows(): pl.pallas_call(functools.partial(gather_kernel, slots, line), out_shape=o...]
where the time goes in v4:
time: 343 us; the launch traced here: 342 us
  Pallas kernels  308 us (90%)
  local copies, waits for them, and re-layouts  23.6 us (7%)
  other arithmetic  5.61 us (2%)
    pallas_call x5, Pallas kernels, gather_rows(): pl.pallas_call(functools.partial(gather_kernel, slots, line), out_shape=o...  174 us
    pallas_call x1, Pallas kernels, factor_inverse(): pl.pallas_call(factor_kernel, out_shape=jax.ShapeDtypeStruct((modes, mode...  69.3 us
    pallas_call x4, Pallas kernels, apply_call(): pl.pallas_call(kernel, grid_spec=pltpu.PrefetchScalarGridSpec(num_scalar_...  34.9 us
    pallas_call x1, Pallas kernels, reduce_sums(): pl.pallas_call(reduce_kernel, out_shape=jax.ShapeDtypeStruct((groups, *su...  24.3 us
    unnamed x24, local copies, waits for them, and re-layouts  19.8 us

profile of v4, /device:TPU:0, one launch (start us, length us, event | category | flops | bytes accessed | tf_op | source)
XLA Modules:
  0.0 341.7 jit_solution(16530140848369675573)
XLA Ops:
  1.4 1.3 fusion.6
  5.6 1.9 copy.12
  7.9 1.2 fusion.7
  9.1 33.0 %gather_rows.4.blocks_ref = bf16[192,128,128]{2,1,0:T(8,128)(2,1)} custom-call(bf16[24,128,128]{2,1,0:T(8,128)(2,1)} %get-tuple-element.20.own_ref), custom_call_target="tpu_custom_call" | custom-call | tf_op jit(solution)/shard_map/gather_rows/pallas_call | solution.py:170
  42.1 2.8 copy-done.2
  44.8 8.2 %shard_map.59 = (f32[24,128,128]{2,1,0:T(8,128)S(1)}, bf16[24,128,128]{2,1,0:T(8,128)(2,1)S(1)}) custom-call(s32[24,27]{1,0:T(8,128)S(1)} %add_subtract_fusion.positions, s32[1]{0:T(128)} %bitcast.own_count, bf16[192,128,128]{2,1,0:T(8,128)(2,1)S(1)} %copy-done.2, bf16[24,27,128,128]{3,2,1,0:T(8,128)(2,1)} %stiff_ref.7, ...), custom_call_target="tpu_custom_call" | custom-call | tf_op jit(solution)/shard_map/pallas_call | solution.py:316
  53.9 35.8 %gather_rows.5.blocks_ref = bf16[192,128,128]{2,1,0:T(8,128)(2,1)} custom-call(bf16[24,128,128]{2,1,0:T(8,128)(2,1)} %copy-done.10), custom_call_target="tpu_custom_call" | custom-call | tf_op jit(solution)/shard_map/gather_rows/pallas_call | solution.py:170
  89.7 2.8 copy-done.1
  92.5 8.2 %shard_map.60 = (f32[24,128,128]{2,1,0:T(8,128)S(1)}, bf16[24,128,128]{2,1,0:T(8,128)(2,1)S(1)}) custom-call(s32[24,27]{1,0:T(8,128)S(1)} %add_subtract_fusion.positions, s32[1]{0:T(128)} %bitcast.own_count, bf16[192,128,128]{2,1,0:T(8,128)(2,1)S(1)} %copy-done.1, bf16[24,27,128,128]{3,2,1,0:T(8,128)(2,1)} %stiff_ref.7, ...), custom_call_target="tpu_custom_call" | custom-call | tf_op jit(solution)/shard_map/pallas_call | solution.py:316
  100.7 1.1 copy-done.7
  102.7 33.1 %gather_rows.6.blocks_ref = bf16[192,128,128]{2,1,0:T(8,128)(2,1)} custom-call(bf16[24,128,128]{2,1,0:T(8,128)(2,1)} %copy-done.9), custom_call_target="tpu_custom_call" | custom-call | tf_op jit(solution)/shard_map/gather_rows/pallas_call | solution.py:170
  135.9 2.8 copy-done
  138.7 9.6 %shard_map.61 = (f32[24,128,128]{2,1,0:T(8,128)}, bf16[24,128,128]{2,1,0:T(8,128)(2,1)S(1)}) custom-call(s32[24,27]{1,0:T(8,128)S(1)} %add_subtract_fusion.positions, s32[1]{0:T(128)} %bitcast.own_count, bf16[192,128,128]{2,1,0:T(8,128)(2,1)S(1)} %copy-done, bf16[24,27,128,128]{3,2,1,0:T(8,128)(2,1)} %stiff_ref.7, f32[24,128,128]{2,1,0:T(8,128)S(1)} %copy-done.8, ...), custom_call_target="tpu_custom_call" | custom-call | tf_op jit(solution)/shard_map/pallas_call | solution.py:316
  149.1 57.4 %gather_both.1 = (bf16[192,128,128]{2,1,0:T(8,128)(2,1)}, bf16[4,24,128,128]{3,2,1,0:T(8,128)(2,1)}) custom-call(bf16[24,128,128]{2,1,0:T(8,128)(2,1)} %copy-done.5), custom_call_target="tpu_custom_call" | custom-call | tf_op jit(solution)/shard_map/gather_both/pallas_call | solution.py:170
  206.6 1.9 copy-done.3
  208.5 2.8 copy-done.4
  211.2 1.1 copy-done.6
  212.4 8.9 %shard_map.62 = f32[256,512]{1,0:T(8,128)S(1)} custom-call(s32[24,27]{1,0:T(8,128)S(1)} %add_subtract_fusion.positions, s32[1]{0:T(128)} %bitcast.own_count, bf16[192,128,128]{2,1,0:T(8,128)(2,1)S(1)} %copy-done.4, bf16[24,27,128,128]{3,2,1,0:T(8,128)(2,1)} %stiff_ref.7, bf16[24,128,128]{2,1,0:T(8,128)(2,1)S(1)} %copy-done.6, ...), custom_call_target="tpu_custom_call" | custom-call | tf_op jit(solution)/shard_map/pallas_call | solution.py:316
  222.1 24.3 %reduce_sums.1 = f32[4,2,16,512]{3,2,1,0:T(8,128)} custom-call(f32[8,2,16,512]{3,2,1,0:T(8,128)} %bitcast.29), custom_call_target="tpu_custom_call" | custom-call | tf_op jit(solution)/shard_map/reduce_sums/pallas_call | solution.py:235
  246.5 14.9 %gather_rows.7 = f32[64,16,512]{2,1,0:T(8,128)} custom-call(f32[8,16,512]{2,1,0:T(8,128)} %bitcast.30), custom_call_target="tpu_custom_call" | custom-call | tf_op jit(solution)/shard_map/gather_rows/pallas_call | solution.py:170
  261.4 1.8 fusion.8
  263.5 69.3 %factor_inverse.1 = f32[512,512]{1,0:T(8,128)S(1)} custom-call(f32[512,512]{1,0:T(8,128)S(1)} %bitcast_add_fusion.gram_ref), custom_call_target="tpu_custom_call" | custom-call | tf_op jit(solution)/shard_map/factor_inverse/pallas_call | solution.py:432
  333.5 1.9 convolution_divide_fusion
  336.1 5.6 %shard_map.63 = f32[128,3072]{1,0:T(8,128)} custom-call(bf16[128,512]{1,0:T(8,128)(2,1)} %dynamic-slice_convert_fusion.rows_ref, bf16[4,24,128,128]{3,2,1,0:T(8,128)(2,1)} %get-tuple-element.15.all_ref), custom_call_target="tpu_custom_call" | custom-call | tf_op jit(solution)/shard_map/pallas_call | solution.py:525
  (26 shorter events, 8.6 us)
Async XLA Ops:
  42.1 2.8 copy-start.2
  53.0 0.9 copy-start.10
  89.7 2.8 copy-start.1
  100.7 1.1 copy-start.7
  101.9 0.9 copy-start.9
  102.7 33.1 %copy-start.8 = (f32[24,128,128]{2,1,0:T(8,128)S(1)}, f32[24,128,128]{2,1,0:T(8,128)}, u32[]{:S(2)}) copy-start(f32[24,128,128]{2,1,0:T(8,128)} %copy-done.7) | copy-start | bytes 4718596
  135.9 2.8 copy-start
  148.3 0.9 copy-start.5
  206.6 1.9 copy-start.3
  208.5 2.8 copy-start.4
  211.2 1.1 copy-start.6
